TPU v7x, 512 devices: a whole 4x8x8 slice. The times are simulated.
512 devices in a mesh: kpool: 16 (over z_hi, x, core), fft: 32 (over z_lo, y).
Axes of the slice: x: 4, y: 8, z: 8 (z_hi: 2, z_lo: 4; z = z_hi * 4 + z_lo), core: 2. Of those that a mesh axis runs over, the one named last changes fastest.
Arguments:
- coeff: bfloat16 [32, 2048, 1536], P('kpool', 'fft'), may hold values from -0.009765625 to 0.009765625
- col_map: int32 [32, 2048], P('kpool'), may hold values from 0 to 9215, as said below
- eigen: float32 [32, 2048], P('kpool'), may hold values from -2 to 2
- band_ids: int32 [8], replicated, may hold values from 0 to 2047, as said below
- tet_corners: int32 [192, 4], replicated, may hold values from 0 to 31, as said below
Outputs:
- density: float32 [192, 9216], P('fft', 'kpool')
Inputs may be any that keep to these rules, and one draw needn't show every extreme that they name: `col_map`: each row holds 2048 distinct positions. `band_ids`: distinct bands. `tet_corners`: the four corners of a tetrahedron are distinct k-points, and every k-point is a corner of some tetrahedron.
All inputs are finite; a program needn't handle non-finite values.
Results may differ from a plain program's by a relative error of at most 0.0003.
The roundings to bfloat16 on the way count: a program that leaves them out, or rounds other values in their place, can miss the bound.
Values may be sent and summed in bfloat16 or wider, within the bound.
A program may use at most 64 MiB of HBM per device.

v0:
```python
import math

import jax
import jax.numpy as jnp
from jax import lax
from jax.sharding import PartitionSpec as P

NX = 96
NY = 96
NZ = 192
ZPW = 96


FERMI_LEVEL = 0.0
SMEARING = 0.1


def phase_table(frequencies, positions, period):
    product = frequencies[:, None] % period * positions[None, :] % period
    phases = 2.0 * math.pi / period * product.astype(jnp.float32)
    cosine = jnp.cos(phases)
    sine_part = jnp.sin(phases)
    upper = jnp.stack([cosine, sine_part], axis=-1)
    lower = jnp.stack([-sine_part, cosine], axis=-1)
    return jnp.stack([upper, lower], axis=1).astype(jnp.bfloat16)


def tetra_weights(levels, corners):
    kpoint_count = levels.shape[0]
    tetra_count = corners.shape[0]
    corner_levels = levels[corners]
    mean_level = jnp.mean(corner_levels, axis=1)
    occupied = jax.nn.sigmoid((FERMI_LEVEL - mean_level) / SMEARING)
    repeated = jnp.repeat(occupied, 4, axis=0)
    onehot = (
        corners.reshape(-1)[:, None] == jnp.arange(kpoint_count, dtype=jnp.int32)[None, :]
    ).astype(jnp.float32)
    summed = jnp.dot(onehot.T, repeated, precision=lax.Precision.HIGHEST)
    return summed * (2.0 / (4 * tetra_count))


def item_density(received, column_map, y_table, x_table):
    planes = received.shape[1] // 2
    dense_grid = (
        jnp.zeros((received.shape[1], NX * NY), received.dtype).at[:, column_map].set(received.T)
    )
    dense_grid = dense_grid.reshape(planes, 2, NX, NY)
    along_y = jnp.einsum(
        "pcxy,ycYC->pxCY", dense_grid, y_table, preferred_element_type=jnp.float32
    ).astype(jnp.bfloat16)
    along_x = jnp.einsum("pxCY,xCXD->pDXY", along_y, x_table, preferred_element_type=jnp.float32)
    return jnp.sum(along_x * along_x, axis=1).reshape(planes, NX * NY)


def per_device(coeff, col_map, eigen, band_ids, tet_corners):
    kpoint_pool = coeff.shape[0]
    column_count = coeff.shape[1]
    band_count = coeff.shape[2] // (2 * ZPW)
    band_levels = jnp.take(eigen, band_ids, axis=1)
    every_level = lax.all_gather(band_levels, "kpool", axis=0, tiled=True)
    weights = tetra_weights(every_level, tet_corners)
    own_weights = lax.dynamic_slice_in_dim(
        weights, lax.axis_index("kpool") * kpoint_pool, kpoint_pool, 0
    )
    slots = jnp.arange(ZPW, dtype=jnp.int32) - ZPW // 2
    z_table = phase_table(slots, jnp.arange(NZ, dtype=jnp.int32), NZ).reshape(2 * ZPW, 2 * NZ)
    y_table = phase_table(jnp.arange(NY, dtype=jnp.int32), jnp.arange(NY, dtype=jnp.int32), NY)
    x_table = phase_table(jnp.arange(NX, dtype=jnp.int32), jnp.arange(NX, dtype=jnp.int32), NX)
    item_count = kpoint_pool * band_count
    coeff_split = coeff.reshape(kpoint_pool, column_count, band_count, 2 * ZPW)
    columns = jnp.einsum(
        "kcbs,sz->kbcz", coeff_split, z_table, preferred_element_type=jnp.float32
    ).astype(jnp.bfloat16)
    columns = columns.reshape(item_count, column_count, 2 * NZ)
    planes = NZ // lax.axis_size("fft")
    start = jnp.zeros((planes, NX * NY), jnp.float32)

    def weighted(position, received):
        kpoint = position // band_count
        band = position % band_count
        return own_weights[kpoint, band] * item_density(received, col_map[kpoint], y_table, x_table)

    def advance(running, position):
        chosen = lax.dynamic_index_in_dim(columns, position, 0, keepdims=False)
        received = lax.all_to_all(chosen, "fft", split_axis=1, concat_axis=0, tiled=True)
        return (running + weighted(position, received), None)

    density, unused = lax.scan(advance, start, jnp.arange(item_count, dtype=jnp.int32))
    summed = lax.psum(density, "kpool")
    share = summed.shape[1] // lax.axis_size("kpool")
    return lax.dynamic_slice_in_dim(summed, lax.axis_index("kpool") * share, share, 1)


def solution(mesh):
    in_specs = (P("kpool", "fft", None), P("kpool", None), P("kpool", None), P(), P())
    out_specs = P("fft", "kpool")
    return jax.shard_map(
        per_device, mesh=mesh, in_specs=in_specs, out_specs=out_specs, check_vma=False
    )
```

profile of v0, /device:TPU:1, one launch (start us, length us, event | category | flops | bytes accessed | tf_op | source)
XLA Modules:
  0.0 712.9 jit_solution(9129507109077147444)
XLA Ops:
  10.4 6.7 copy.82
  17.1 14.5 %reshape.324 = bf16[192,384,1,1]{1,0,2,3:T(8,128)(2,1)S(1)} reshape(bf16[96,2,192,2]{3,2,1,0:T(8,128)(2,1)} %copy.82) | data formatting | bytes 294912 | tf_op jit(solution)/shard_map/convert_element_type | solution.py:25
  33.2 36.2 %all-gather = f32[16,2,8]{2,1,0:T(2,128)S(1)} all-gather(f32[1,2,8]{2,1,0:T(2,128)S(1)} %bitcast.108), channel_id=1, replica_groups=mesh['kpool'=16,'fft'=32] {'kpool'}, dimensions={0}, use_global_device_ids=true | all-gather | bytes 1088 | tf_op jit(solution)/shard_map/all_gather | solution.py:60
  69.7 1.6 gather_fusion.1
  71.8 1.3 convolution_convert_fusion
  73.9 446.1 %while.14 = (s32[]{:T(128)}, f32[6,9216]{1,0:T(8,128)S(1)}, s32[16]{0:T(128)S(1)}, f32[2,8]{1,0:T(2,128)S(1)}, s32[2,2048]{1,0:T(2,128)S(1)}, /*index=5*/bf16[16...) while((s32[]{:T(128)}, f32[6,9216]{1,0:T(8,128)S(1)}, ...), condition=%wide.region_4.5_spmd.clone, body=%wide.region_1.0_spmd.clone.sunk | while | flops 85383192 | bytes 4465149 | solution.py:88
  78.3 9.9 %all-to-all-start = ((bf16[32,2,384]{2,1,0:T(2,128)(2,1)}), bf16[32,2,384]{2,1,0:T(2,128)(2,1)S(1)}, u32[]{:S(2)}, u32[]{:S(2)}) async-start(bf16[32,2,384]{2,1,0:T(2,128)(2,1)} %reshape.338), calls=%async_computation | async-start | bytes 98304 | tf_op jit(solution)/shard_map/while/body/eval_jaxpr/all_to_all | solution.py:85
  91.0 6.3 all-to-all-done
  97.8 6.6 scatter_custom_fusion.6
  104.5 1.0 copy.104
  111.9 3.8 all-to-all-start
  118.5 6.3 all-to-all-done
  125.3 6.6 scatter_custom_fusion.6
  132.0 1.0 copy.104
  139.4 3.8 all-to-all-start
  146.0 6.3 all-to-all-done
  152.8 6.6 scatter_custom_fusion.6
  159.5 1.0 copy.104
  166.9 3.8 all-to-all-start
  173.5 6.3 all-to-all-done
  180.3 6.6 scatter_custom_fusion.6
  187.0 1.0 copy.104
  194.4 3.8 all-to-all-start
  201.0 6.3 all-to-all-done
  207.8 6.6 scatter_custom_fusion.6
  214.5 1.0 copy.104
  221.9 3.8 all-to-all-start
  228.5 6.3 all-to-all-done
  235.3 6.6 scatter_custom_fusion.6
  242.0 1.0 copy.104
  249.4 3.8 all-to-all-start
  256.0 6.3 all-to-all-done
  262.8 6.6 scatter_custom_fusion.6
  269.5 1.0 copy.104
  276.9 3.8 all-to-all-start
  283.5 6.3 all-to-all-done
  290.3 6.6 scatter_custom_fusion.6
  297.0 1.0 copy.104
  304.4 3.8 all-to-all-start
  311.0 6.3 all-to-all-done
  317.8 6.6 scatter_custom_fusion.6
  331.9 3.8 all-to-all-start
  338.5 6.3 all-to-all-done
  345.3 6.6 scatter_custom_fusion.6
  359.4 3.8 all-to-all-start
  366.0 6.3 all-to-all-done
  372.8 6.6 scatter_custom_fusion.6
  386.9 3.8 all-to-all-start
  393.5 6.3 all-to-all-done
  400.3 6.6 scatter_custom_fusion.6
  414.4 3.8 all-to-all-start
  421.0 6.3 all-to-all-done
  427.8 6.6 scatter_custom_fusion.6
  441.9 3.8 all-to-all-start
  448.5 6.3 all-to-all-done
  455.3 6.6 scatter_custom_fusion.6
  469.4 3.8 all-to-all-start
  476.0 6.3 all-to-all-done
  482.8 6.6 scatter_custom_fusion.6
  496.9 3.8 all-to-all-start
  503.5 6.3 all-to-all-done
  510.3 6.6 scatter_custom_fusion.6
  520.8 183.8 %all-reduce.2.cloned.1.call-done = f32[6,9216]{1,0:T(8,128)} async-done(((f32[6,9216]{1,0:T(8,128)}), f32[6,9216]{1,0:T(8,128)}) %all-reduce.2.cloned.1.call-update) | async-done | bytes 221200 | tf_op jit(solution)/shard_map/psum | solution.py:89
  704.6 1.4 constant_dynamic-slice_fusion.1
  (305 shorter events, 103.9 us)
Async XLA Ops:
  6.5 698.1 %all-reduce.2.cloned.1.call-start = ((), (), s32[]{:S(2)}) async-start(), calls=%async_computation.1 | async-start | bytes 589824 | tf_op jit(solution)/shard_map/psum | solution.py:89
  17.1 14.5 %copy-start.1 = (bf16[2,64,1536]{2,1,0:T(8,128)(2,1)S(1)}, bf16[2,64,1536]{2,1,0:T(8,128)(2,1)}, u32[]{:S(2)}) copy-start(bf16[2,64,1536]{2,1,0:T(8,128)(2,1)} %param.7) | copy-start | bytes 1179652
  17.1 14.9 %copy-start.3 = (f32[2,2048]{1,0:T(2,128)S(1)}, f32[2,2048]{1,0:T(2,128)}, u32[]{:S(2)}) copy-start(f32[2,2048]{1,0:T(2,128)} %param.9) | copy-start | bytes 49156
  71.2 2.7 copy-start.2
  78.3 19.0 %all-to-all-start = ((bf16[32,2,384]{2,1,0:T(2,128)(2,1)}), bf16[32,2,384]{2,1,0:T(2,128)(2,1)S(1)}, u32[]{:S(2)}, u32[]{:S(2)}) async-start(bf16[32,2,384]{2,1,0:T(2,128)(2,1)} %reshape.338), calls=%async_computation | async-start | bytes 98304 | tf_op jit(solution)/shard_map/while/body/eval_jaxpr/all_to_all | solution.py:85
  111.9 12.9 %all-to-all-start = ((bf16[32,2,384]{2,1,0:T(2,128)(2,1)}), bf16[32,2,384]{2,1,0:T(2,128)(2,1)S(1)}, u32[]{:S(2)}, u32[]{:S(2)}) async-start(bf16[32,2,384]{2,1,0:T(2,128)(2,1)} %reshape.338), calls=%async_computation | async-start | bytes 98304 | tf_op jit(solution)/shard_map/while/body/eval_jaxpr/all_to_all | solution.py:85
  139.4 12.9 %all-to-all-start = ((bf16[32,2,384]{2,1,0:T(2,128)(2,1)}), bf16[32,2,384]{2,1,0:T(2,128)(2,1)S(1)}, u32[]{:S(2)}, u32[]{:S(2)}) async-start(bf16[32,2,384]{2,1,0:T(2,128)(2,1)} %reshape.338), calls=%async_computation | async-start | bytes 98304 | tf_op jit(solution)/shard_map/while/body/eval_jaxpr/all_to_all | solution.py:85
  166.9 12.9 %all-to-all-start = ((bf16[32,2,384]{2,1,0:T(2,128)(2,1)}), bf16[32,2,384]{2,1,0:T(2,128)(2,1)S(1)}, u32[]{:S(2)}, u32[]{:S(2)}) async-start(bf16[32,2,384]{2,1,0:T(2,128)(2,1)} %reshape.338), calls=%async_computation | async-start | bytes 98304 | tf_op jit(solution)/shard_map/while/body/eval_jaxpr/all_to_all | solution.py:85
  194.4 12.9 %all-to-all-start = ((bf16[32,2,384]{2,1,0:T(2,128)(2,1)}), bf16[32,2,384]{2,1,0:T(2,128)(2,1)S(1)}, u32[]{:S(2)}, u32[]{:S(2)}) async-start(bf16[32,2,384]{2,1,0:T(2,128)(2,1)} %reshape.338), calls=%async_computation | async-start | bytes 98304 | tf_op jit(solution)/shard_map/while/body/eval_jaxpr/all_to_all | solution.py:85
  221.9 12.9 %all-to-all-start = ((bf16[32,2,384]{2,1,0:T(2,128)(2,1)}), bf16[32,2,384]{2,1,0:T(2,128)(2,1)S(1)}, u32[]{:S(2)}, u32[]{:S(2)}) async-start(bf16[32,2,384]{2,1,0:T(2,128)(2,1)} %reshape.338), calls=%async_computation | async-start | bytes 98304 | tf_op jit(solution)/shard_map/while/body/eval_jaxpr/all_to_all | solution.py:85
  249.4 12.9 %all-to-all-start = ((bf16[32,2,384]{2,1,0:T(2,128)(2,1)}), bf16[32,2,384]{2,1,0:T(2,128)(2,1)S(1)}, u32[]{:S(2)}, u32[]{:S(2)}) async-start(bf16[32,2,384]{2,1,0:T(2,128)(2,1)} %reshape.338), calls=%async_computation | async-start | bytes 98304 | tf_op jit(solution)/shard_map/while/body/eval_jaxpr/all_to_all | solution.py:85
  276.9 12.9 %all-to-all-start = ((bf16[32,2,384]{2,1,0:T(2,128)(2,1)}), bf16[32,2,384]{2,1,0:T(2,128)(2,1)S(1)}, u32[]{:S(2)}, u32[]{:S(2)}) async-start(bf16[32,2,384]{2,1,0:T(2,128)(2,1)} %reshape.338), calls=%async_computation | async-start | bytes 98304 | tf_op jit(solution)/shard_map/while/body/eval_jaxpr/all_to_all | solution.py:85
  304.4 12.9 %all-to-all-start = ((bf16[32,2,384]{2,1,0:T(2,128)(2,1)}), bf16[32,2,384]{2,1,0:T(2,128)(2,1)S(1)}, u32[]{:S(2)}, u32[]{:S(2)}) async-start(bf16[32,2,384]{2,1,0:T(2,128)(2,1)} %reshape.338), calls=%async_computation | async-start | bytes 98304 | tf_op jit(solution)/shard_map/while/body/eval_jaxpr/all_to_all | solution.py:85
  331.9 12.9 %all-to-all-start = ((bf16[32,2,384]{2,1,0:T(2,128)(2,1)}), bf16[32,2,384]{2,1,0:T(2,128)(2,1)S(1)}, u32[]{:S(2)}, u32[]{:S(2)}) async-start(bf16[32,2,384]{2,1,0:T(2,128)(2,1)} %reshape.338), calls=%async_computation | async-start | bytes 98304 | tf_op jit(solution)/shard_map/while/body/eval_jaxpr/all_to_all | solution.py:85
  359.4 12.9 %all-to-all-start = ((bf16[32,2,384]{2,1,0:T(2,128)(2,1)}), bf16[32,2,384]{2,1,0:T(2,128)(2,1)S(1)}, u32[]{:S(2)}, u32[]{:S(2)}) async-start(bf16[32,2,384]{2,1,0:T(2,128)(2,1)} %reshape.338), calls=%async_computation | async-start | bytes 98304 | tf_op jit(solution)/shard_map/while/body/eval_jaxpr/all_to_all | solution.py:85
  386.9 12.9 %all-to-all-start = ((bf16[32,2,384]{2,1,0:T(2,128)(2,1)}), bf16[32,2,384]{2,1,0:T(2,128)(2,1)S(1)}, u32[]{:S(2)}, u32[]{:S(2)}) async-start(bf16[32,2,384]{2,1,0:T(2,128)(2,1)} %reshape.338), calls=%async_computation | async-start | bytes 98304 | tf_op jit(solution)/shard_map/while/body/eval_jaxpr/all_to_all | solution.py:85
  414.4 12.9 %all-to-all-start = ((bf16[32,2,384]{2,1,0:T(2,128)(2,1)}), bf16[32,2,384]{2,1,0:T(2,128)(2,1)S(1)}, u32[]{:S(2)}, u32[]{:S(2)}) async-start(bf16[32,2,384]{2,1,0:T(2,128)(2,1)} %reshape.338), calls=%async_computation | async-start | bytes 98304 | tf_op jit(solution)/shard_map/while/body/eval_jaxpr/all_to_all | solution.py:85
  441.9 12.9 %all-to-all-start = ((bf16[32,2,384]{2,1,0:T(2,128)(2,1)}), bf16[32,2,384]{2,1,0:T(2,128)(2,1)S(1)}, u32[]{:S(2)}, u32[]{:S(2)}) async-start(bf16[32,2,384]{2,1,0:T(2,128)(2,1)} %reshape.338), calls=%async_computation | async-start | bytes 98304 | tf_op jit(solution)/shard_map/while/body/eval_jaxpr/all_to_all | solution.py:85
  469.4 12.9 %all-to-all-start = ((bf16[32,2,384]{2,1,0:T(2,128)(2,1)}), bf16[32,2,384]{2,1,0:T(2,128)(2,1)S(1)}, u32[]{:S(2)}, u32[]{:S(2)}) async-start(bf16[32,2,384]{2,1,0:T(2,128)(2,1)} %reshape.338), calls=%async_computation | async-start | bytes 98304 | tf_op jit(solution)/shard_map/while/body/eval_jaxpr/all_to_all | solution.py:85
  496.9 12.9 %all-to-all-start = ((bf16[32,2,384]{2,1,0:T(2,128)(2,1)}), bf16[32,2,384]{2,1,0:T(2,128)(2,1)S(1)}, u32[]{:S(2)}, u32[]{:S(2)}) async-start(bf16[32,2,384]{2,1,0:T(2,128)(2,1)} %reshape.338), calls=%async_computation | async-start | bytes 98304 | tf_op jit(solution)/shard_map/while/body/eval_jaxpr/all_to_all | solution.py:85
  520.0 0.7 copy-start
Sparse Core Ops, SparseCore 0:
  520.9 183.6 all-reduce.1
where the time goes:
time: 717 us; the launch traced here: 713 us
  waiting for transfers between devices  285 us (40%)
  local copies, waits for them, and re-layouts  216 us (30%)
  starting transfers between devices  67.5 us (9%)
  loops' own time  67 us (9%)
  blocking collectives  36.2 us (5%)
  other arithmetic  16.6 us (2%)
  between operations  13.6 us (2%)
  matrix products  10.6 us (1%)
    psum x1, waiting for transfers between devices, per_device(): summed = lax.psum(density, 'kpool')  184 us
    scatter x32, local copies, waits for them, and re-layouts, item_density(): jnp.zeros((received.shape[1], NX * NY), received.dtype).at[:, column_map]  122 us
    all_to_all x16, waiting for transfers between devices, advance(): lax.all_to_all(chosen, 'fft', split_axis=1, concat_axis=0, tiled=True)  101 us
    all_to_all x16, starting transfers between devices, advance(): lax.all_to_all(chosen, 'fft', split_axis=1, concat_axis=0, tiled=True)  67.5 us
    another operation x1, loops' own time, per_device(): lax.scan(advance, start, jnp.arange(item_count, dtype=jnp.int32))  67 us
    all_gather x1, blocking collectives, per_device(): every_level = lax.all_gather(band_levels, 'kpool', axis=0, tiled=True)  36.2 us
    dynamic_slice x32, local copies, waits for them, and re-layouts, advance(): chosen = lax.dynamic_index_in_dim(columns, position, 0, keepdims=False)  14.9 us
    convert_element_type x1, local copies, waits for them, and re-layouts, phase_table(): return jnp.stack([upper, lower], axis=1).astype(jnp.bfloat16)  14.5 us
  transfers between devices with their start and end apart: 17, of which 17 were waited for; matrix products, arithmetic and copies ran while one was open for 2% of the time, Pallas kernels for 0%

commit v1 on v0

v1 whole, which is shorter than its diff:
```python
import functools

import jax
import jax.numpy as jnp
import ml_dtypes
import numpy as np
from jax import lax
from jax.experimental import pallas as pl
from jax.experimental.pallas import tpu as pltpu
from jax.sharding import PartitionSpec as P

NX = 96
NY = 96
NZ = 192
ZPW = 96
BANDS = 8
COLS = 2048
KPOINTS = 32
NTET = 192

FFT = 32
POOLS = 16
KP = 2
LOCAL = COLS // FFT
PLANES = NZ // FFT
ROWS = 48
SMEARING = 0.1
MESH = pl.DeviceIdType.MESH
F32 = jnp.float32
BF16 = jnp.bfloat16
NT = (((1,), (1,)), ((), ()))


def phase_parts(frequencies, positions, period):
    product = frequencies[:, None] % period * positions[None, :] % period
    phases = np.float32(2.0 * np.pi / period) * product.astype(np.float32)
    return np.cos(phases), np.sin(phases)


def z_matrices():
    cosine, sine = phase_parts(np.arange(ZPW) - ZPW // 2, np.arange(NZ), NZ)
    full = np.zeros((ZPW, 2, NZ, 2), np.float32)
    full[:, 0, :, 0] = cosine
    full[:, 0, :, 1] = sine
    full[:, 1, :, 0] = -sine
    full[:, 1, :, 1] = cosine
    full = full.reshape(2 * ZPW, FFT, PLANES * 2).transpose(1, 2, 0)
    result = np.zeros((3, FFT, 8, 2, 2 * ZPW), np.float32)
    result[0, :, :, 0] = full[:, :8]
    result[1, :, :, 1] = full[:, :8]
    result[2, :, :4, 0] = full[:, 8:]
    result[2, :, 4:, 1] = full[:, 8:]
    return result.reshape(3, FFT * 8, 4 * ZPW).astype(ml_dtypes.bfloat16)


def y_matrix():
    cosine, sine = phase_parts(np.arange(NY), np.arange(NY), NY)
    result = np.zeros((2, 128, 2, 128), np.float32)
    result[0, :NY, 0, :NY] = cosine
    result[0, :NY, 1, :NY] = sine
    result[1, :NY, 0, :NY] = -sine
    result[1, :NY, 1, :NY] = cosine
    return result.reshape(256, 256).astype(ml_dtypes.bfloat16)


def x_matrix():
    cosine, sine = phase_parts(np.arange(NX), np.arange(NX), NX)
    result = np.zeros((2, 2, 4, 2, 8, 2, NX), np.float32)
    for core in range(2):
        for chip in range(4):
            for high in range(2):
                owner = (high * 4 + chip) * 2 + core
                mine = slice(owner * 6, owner * 6 + 6)
                result[0, core, chip, high, :6, 0] = cosine[:, mine].T
                result[0, core, chip, high, :6, 1] = -sine[:, mine].T
                result[1, core, chip, high, :6, 0] = sine[:, mine].T
                result[1, core, chip, high, :6, 1] = cosine[:, mine].T
    return result.reshape(256, 2 * NX).astype(ml_dtypes.bfloat16)


def iota(shape, dim):
    return lax.broadcasted_iota(jnp.int32, shape, dim).astype(F32)


def onehot(condition):
    return jnp.where(condition, 1.0, 0.0).astype(BF16)


def dot(a, b):
    return jnp.dot(a, b, preferred_element_type=F32)


def dot_nt(a, b):
    return lax.dot_general(a, b, NT, preferred_element_type=F32)


def wait_bytes(ref, sem):
    pltpu.make_async_copy(ref, ref, sem).wait()


def kernel(
    coeff, col_map, eigen, band_ids, corners, z_mat, y_mat, x_mat, out,
    send, recv, own_levels, levels, level_rows, weights, ranks, places, block_v, block_s,
    sorter, windows, columns, ordered, grid, density, half, in_core, in_x, in_z, quarter,
    send_sem, recv_sem, local_sem, level_sem, core_sem, x_send, x_recv, z_sem,
):
    fft = lax.axis_index("fft")
    pool = lax.axis_index("kpool")
    core = pool % 2
    chip = pool // 2 % 4
    high = pool // 8

    barrier = pltpu.get_barrier_semaphore()

    def greet_fft(step, carry):
        pl.semaphore_signal(
            barrier, inc=1, device_id={"fft": (fft + step) % FFT}, device_id_type=MESH
        )
        return carry

    def greet_pool(step, carry):
        pl.semaphore_signal(
            barrier, inc=1, device_id={"kpool": (pool + step) % POOLS}, device_id_type=MESH
        )
        return carry

    lax.fori_loop(1, FFT, greet_fft, 0)
    lax.fori_loop(1, POOLS, greet_pool, 0)

    def z_step(k):
        groups = []
        for pair in range(2):
            both = jnp.concatenate(
                [coeff[k, :, (2 * h + pair) * 384 : (2 * h + pair + 1) * 384] for h in range(2)],
                axis=0,
            )
            for part in range(3):
                groups.append(dot_nt(z_mat[part], both).reshape(FFT, 8, 128))
        for tile in range(3):
            joined = jnp.concatenate([groups[2 * tile], groups[2 * tile + 1]], axis=1)
            send[k, :, 16 * tile : 16 * tile + 16, :] = joined.astype(BF16)

    def send_columns(k):
        def one(step, carry):
            target = (fft + step) % FFT
            pltpu.make_async_remote_copy(
                src_ref=send.at[k, target],
                dst_ref=recv.at[k, fft],
                send_sem=send_sem.at[k],
                recv_sem=recv_sem.at[k],
                device_id={"fft": target},
                device_id_type=MESH,
            ).start()
            return carry

        lax.fori_loop(1, FFT, one, 0)
        pltpu.make_async_copy(send.at[k, fft], recv.at[k, fft], local_sem.at[k]).start()

    z_step(0)
    pl.semaphore_wait(barrier, FFT - 1 + POOLS - 1)
    send_columns(0)

    lanes = lax.broadcasted_iota(jnp.int32, (KP, 2048), 1)
    lane8 = lax.broadcasted_iota(jnp.int32, (KP, 128), 1)
    table = jnp.zeros((KP, 128), F32)
    for n in range(BANDS):
        picked = jnp.sum(jnp.where(lanes == band_ids[n], eigen[...], 0.0), axis=1, keepdims=True)
        table = jnp.where(lane8 == n, picked, table)
    own_levels[...] = jnp.zeros_like(own_levels)
    own_levels[0:KP, :] = table

    def send_levels(step, carry):
        pltpu.make_async_remote_copy(
            src_ref=own_levels,
            dst_ref=levels.at[pool],
            send_sem=level_sem.at[0],
            recv_sem=level_sem.at[1],
            device_id={"kpool": (pool + step) % POOLS},
            device_id_type=MESH,
        ).start()
        return carry

    lax.fori_loop(1, POOLS, send_levels, 0)
    pltpu.make_async_copy(own_levels, levels.at[pool], local_sem.at[2]).start()

    z_step(1)
    send_columns(1)

    for k in range(KP):
        place = col_map[k : k + 1, :].astype(F32)
        x_of = jnp.floor((place + 0.5) * (1.0 / NY))
        y_of = place - NY * x_of
        rows = iota((128, COLS), 0)
        in_x_row = rows == x_of
        x_hot = onehot(in_x_row)
        y_hot = onehot(rows == y_of)
        taken = dot_nt(x_hot, y_hot)
        first = iota((128, 128), 0)
        second = iota((128, 128), 1)
        taken_b = taken.astype(BF16)
        before = dot(taken_b, onehot(first < second))
        above = dot(onehot(second < first), taken_b)
        start = jnp.sum(above, axis=1, keepdims=True)
        x_from = lax.broadcasted_iota(jnp.int32, (NX, COLS), 0) * NY
        count = jnp.sum(
            jnp.where(col_map[k : k + 1, :] < x_from, 1, 0), axis=1, keepdims=True
        )
        block_v[k] = jnp.broadcast_to(jnp.minimum(count >> 7, COLS // 128 - 1), (NX, 128))
        block = jnp.minimum(jnp.floor(start * (1.0 / 128)), COLS // 128 - 1.0)
        places[k] = jnp.where(taken > 0.5, start + before - 128.0 * block, -1.0)
        within = dot(before.astype(BF16), y_hot)
        ranks[k : k + 1, :] = jnp.sum(
            jnp.where(in_x_row, start + within, 0.0), axis=0, keepdims=True
        )
    block_copy = pltpu.make_async_copy(block_v, block_s, local_sem.at[3])
    block_copy.start()

    for k in range(KP):
        def sorter_rows(step, carry, k=k):
            at = pl.multiple_of(step * 64, 64)
            rows = iota((64, COLS), 0) + (step * 64).astype(F32)
            sorter[k, pl.ds(at, 64), :] = onehot(rows == ranks[k : k + 1, :])
            return carry

        lax.fori_loop(0, COLS // 64, sorter_rows, 0)

        def window(x, carry, k=k):
            windows[k, x] = onehot(iota((256, 128), 0) == places[k, pl.ds(x, 1), :])
            return carry

        lax.fori_loop(0, NX, window, 0)

    wait_bytes(levels.at[pl.ds(0, POOLS - 1)], level_sem.at[1])
    pltpu.make_async_copy(own_levels, levels.at[pool], local_sem.at[2]).wait()
    level_rows[...] = jnp.zeros_like(level_rows)
    for j in range(POOLS):
        level_rows[KP * j : KP * j + KP, :] = levels[j, 0:KP, :]
    kpoint = lax.broadcasted_iota(jnp.int32, (NTET, 128), 1)
    member = jnp.zeros((NTET, 128), F32)
    for c in range(4):
        member = member + jnp.where(corners[:, c : c + 1] == kpoint, 1.0, 0.0)
    mean = 0.25 * jnp.dot(
        member, level_rows[...], precision=lax.Precision.HIGHEST, preferred_element_type=F32
    )
    occupied = jax.nn.sigmoid((0.0 - mean) / SMEARING)
    lane128 = lax.broadcasted_iota(jnp.int32, (1, 128), 1)
    for k in range(KP):
        mine = jnp.sum(
            jnp.where(kpoint == pool * KP + k, member, 0.0), axis=1, keepdims=True
        )
        row = jnp.sum(mine * occupied, axis=0, keepdims=True) * (2.0 / (4 * NTET))
        for n in range(BANDS):
            value = jnp.sum(jnp.where(lane128 == n, row, 0.0), axis=1, keepdims=True)
            weights[k * BANDS + n : k * BANDS + n + 1, :] = jnp.broadcast_to(value, (1, 128))

    ordered[COLS // 128] = jnp.zeros((2 * ROWS, 128), BF16)
    density[...] = jnp.zeros_like(density)
    block_copy.wait()

    for k in range(KP):
        wait_bytes(recv.at[k, pl.ds(0, FFT - 1)], recv_sem.at[k])
        pltpu.make_async_copy(send.at[k, fft], recv.at[k, fft], local_sem.at[k]).wait()

        def merge(step, carry, k=k):
            even = recv[k, 2 * step].astype(F32)
            odd = recv[k, 2 * step + 1].astype(F32)
            low = lax.broadcasted_iota(jnp.int32, (ROWS, 128), 1) < LOCAL
            at = pl.ds(pl.multiple_of(step * 128, 128), 128)
            columns[0:ROWS, at] = jnp.where(low, even, pltpu.roll(odd, LOCAL, 1)).astype(BF16)
            columns[ROWS:, at] = jnp.where(low, pltpu.roll(even, LOCAL, 1), odd).astype(BF16)
            return carry

        lax.fori_loop(0, FFT // 2, merge, 0, unroll=4)

        def order(step, carry, k=k):
            at = pl.ds(pl.multiple_of(step * 256, 256), 256)
            part = dot_nt(columns[...], sorter[k, at, :]).astype(BF16)
            ordered[2 * step] = part[:, :128]
            ordered[2 * step + 1] = part[:, 128:]
            return carry

        lax.fori_loop(0, COLS // 256, order, 0, unroll=2)

        def grid_row(x, carry, k=k):
            block = block_s[k, x, 0]
            near = jnp.concatenate([ordered[block], ordered[block + 1]], axis=1)
            grid[pl.ds(pl.multiple_of(x * 2 * ROWS, 8), 2 * ROWS), :] = dot(near, windows[k, x])
            return carry

        lax.fori_loop(0, NX, grid_row, 0, unroll=8)

        def band_pair(step, carry, k=k):
            weight = [
                weights[pl.ds(k * BANDS + 2 * step + e, 1), :] for e in range(2)
            ]
            for p in range(PLANES):
                row = step * 24 + (2 * p if p < 4 else 16 + 2 * (p - 4))
                apart = 8 if p < 4 else 4
                field = jnp.concatenate(
                    [
                        jnp.concatenate(
                            [
                                grid[pl.ds(row + apart * e + c, NX, stride=2 * ROWS), :]
                                for c in range(2)
                            ],
                            axis=1,
                        )
                        for e in range(2)
                    ],
                    axis=0,
                ).astype(BF16)
                along_y = dot(field, y_mat[...]).astype(BF16)
                turned = jnp.concatenate(
                    [
                        jnp.concatenate([along_y[:NX, :128], along_y[NX:, :128]], axis=1),
                        jnp.concatenate([along_y[:NX, 128:], along_y[NX:, 128:]], axis=1),
                    ],
                    axis=0,
                )
                psi = dot(x_mat[...], turned)
                power = psi[:128] * psi[:128] + psi[128:] * psi[128:]
                density[p] += weight[0] * power[:, :128] + weight[1] * power[:, 128:]
            return carry

        lax.fori_loop(0, BANDS // 2, band_pair, 0)

    other = pl.ds(pl.multiple_of((1 - core) * 64, 64), 64)
    mine = pl.ds(pl.multiple_of(core * 64, 64), 64)
    core_copy = pltpu.make_async_remote_copy(
        src_ref=density.at[:, other, :],
        dst_ref=in_core,
        send_sem=core_sem.at[0],
        recv_sem=core_sem.at[1],
        device_id={"kpool": pool + 1 - 2 * core},
        device_id_type=MESH,
    )
    core_copy.start()
    core_copy.wait()
    half[...] = density[:, mine, :] + in_core[...]
    x_copies = []
    for step in range(1, 4):
        target = (chip + step) % 4
        copy = pltpu.make_async_remote_copy(
            src_ref=half.at[:, pl.ds(pl.multiple_of(target * 16, 16), 16), :],
            dst_ref=in_x.at[step - 1],
            send_sem=x_send.at[step - 1],
            recv_sem=x_recv.at[step - 1],
            device_id={"kpool": (high * 4 + target) * 2 + core},
            device_id_type=MESH,
        )
        copy.start()
        x_copies.append(copy)
    for copy in x_copies:
        copy.wait()
    quarter[...] = (
        half[:, pl.ds(pl.multiple_of(chip * 16, 16), 16), :] + in_x[0] + in_x[1] + in_x[2]
    )
    z_copy = pltpu.make_async_remote_copy(
        src_ref=quarter.at[:, pl.ds(pl.multiple_of((1 - high) * 8, 8), 8), :],
        dst_ref=in_z,
        send_sem=z_sem.at[0],
        recv_sem=z_sem.at[1],
        device_id={"kpool": pool + 8 - 16 * high},
        device_id_type=MESH,
    )
    z_copy.start()
    z_copy.wait()
    total = quarter[:, pl.ds(pl.multiple_of(high * 8, 8), 8), :] + in_z[...]
    for i in range(6):
        out[:, NY * i : NY * (i + 1)] = total[:, i, :NY]

    for k in range(KP):
        wait_bytes(send.at[k, pl.ds(0, FFT - 1)], send_sem.at[k])
    wait_bytes(levels.at[pl.ds(0, POOLS - 1)], level_sem.at[0])


def per_device(coeff, col_map, eigen, band_ids, tet_corners):
    vmem = pl.BlockSpec(memory_space=pltpu.VMEM)
    smem = pl.BlockSpec(memory_space=pltpu.SMEM)
    return pl.pallas_call(
        kernel,
        out_shape=jax.ShapeDtypeStruct((PLANES, 6 * NY), F32),
        in_specs=[vmem, vmem, vmem, smem, vmem, vmem, vmem, vmem],
        out_specs=vmem,
        scratch_shapes=[
            pltpu.VMEM((KP, FFT, ROWS, 128), BF16),
            pltpu.VMEM((KP, FFT, ROWS, 128), BF16),
            pltpu.VMEM((8, 128), F32),
            pltpu.VMEM((POOLS, 8, 128), F32),
            pltpu.VMEM((128, 128), F32),
            pltpu.VMEM((KP * BANDS, 128), F32),
            pltpu.VMEM((8, COLS), F32),
            pltpu.VMEM((KP, 128, 128), F32),
            pltpu.VMEM((KP, NX, 128), jnp.int32),
            pltpu.SMEM((KP, NX, 128), jnp.int32),
            pltpu.VMEM((KP, COLS, COLS), BF16),
            pltpu.VMEM((KP, NX, 256, 128), BF16),
            pltpu.VMEM((2 * ROWS, COLS), BF16),
            pltpu.VMEM((COLS // 128 + 1, 2 * ROWS, 128), BF16),
            pltpu.VMEM((NX * 2 * ROWS, 128), F32),
            pltpu.VMEM((PLANES, 128, 128), F32),
            pltpu.VMEM((PLANES, 64, 128), F32),
            pltpu.VMEM((PLANES, 64, 128), F32),
            pltpu.VMEM((3, PLANES, 16, 128), F32),
            pltpu.VMEM((PLANES, 8, 128), F32),
            pltpu.VMEM((PLANES, 16, 128), F32),
            pltpu.SemaphoreType.DMA((KP,)),
            pltpu.SemaphoreType.DMA((KP,)),
            pltpu.SemaphoreType.DMA((4,)),
            pltpu.SemaphoreType.DMA((2,)),
            pltpu.SemaphoreType.DMA((2,)),
            pltpu.SemaphoreType.DMA((3,)),
            pltpu.SemaphoreType.DMA((3,)),
            pltpu.SemaphoreType.DMA((2,)),
        ],
        compiler_params=pltpu.CompilerParams(
            collective_id=0, has_side_effects=True, vmem_limit_bytes=56 * 1024 * 1024
        ),
    )(
        coeff, col_map, eigen, band_ids, tet_corners,
        jnp.asarray(z_matrices()), jnp.asarray(y_matrix()), jnp.asarray(x_matrix()),
    )


def solution(mesh):
    in_specs = (P("kpool", "fft", None), P("kpool", None), P("kpool", None), P(), P())
    out_specs = P("fft", "kpool")
    return jax.shard_map(
        per_device, mesh=mesh, in_specs=in_specs, out_specs=out_specs, check_vma=False
    )
```

time: 717 us -> 73.6 us (0.10)
  waiting for transfers between devices: 285 us -> 0 us
  local copies, waits for them, and re-layouts: 216 us -> 2.77 us
  Pallas kernels: 0 us -> 70.6 us
  starting transfers between devices: 67.5 us -> 0 us
  loops' own time: 67 us -> 0 us
  blocking collectives: 36.2 us -> 0 us
  other arithmetic: 16.6 us -> 0 us
  between operations: 13.6 us -> 0.01 us
  matrix products: 10.6 us -> 0 us
    psum x1 -> x0, waiting for transfers between devices: 184 us -> none  [per_device(): summed = lax.psum(density, 'kpool')]
    scatter x32 -> x0, local copies, waits for them, and re-layouts: 122 us -> none  [item_density(): jnp.zeros((received.shape[1], NX * NY), received.dtype).at[:, column_map]]
    all_to_all x16 -> x0, waiting for transfers between devices: 101 us -> none  [advance(): lax.all_to_all(chosen, 'fft', split_axis=1, concat_axis=0, tiled=True)]
    pallas_call x0 -> x1, Pallas kernels: none -> 70.6 us  [per_device(): pl.pallas_call(kernel, out_shape=jax.ShapeDtypeStruct((PLANES, 6 * NY), F...]
    all_to_all x16 -> x0, starting transfers between devices: 67.5 us -> none  [advance(): lax.all_to_all(chosen, 'fft', split_axis=1, concat_axis=0, tiled=True)]
    another operation x1 -> x0, loops' own time: 67 us -> none  [per_device(): lax.scan(advance, start, jnp.arange(item_count, dtype=jnp.int32))]
    dynamic_slice x65 -> x0, local copies, waits for them, and re-layouts: 37.2 us -> none  [the longest x32 14.9 us: advance(): chosen = lax.dynamic_index_in_dim(columns, position, 0, keepdims=False)]
    all_gather x1 -> x0, blocking collectives: 36.2 us -> none  [per_device(): every_level = lax.all_gather(band_levels, 'kpool', axis=0, tiled=True)]
  transfers between devices with their start and end apart: 17 -> 0, of which waited for: 17 -> 0; matrix products, arithmetic and copies ran while one was open for 2% -> 0% of each run, Pallas kernels for 0% -> 0%
where the time goes in v1:
time: 73.6 us; the launch traced here: 73.3 us
  Pallas kernels  70.6 us (96%)
  local copies, waits for them, and re-layouts  2.77 us (4%)
    pallas_call x1, Pallas kernels, per_device(): pl.pallas_call(kernel, out_shape=jax.ShapeDtypeStruct((PLANES, 6 * NY), F...  70.6 us
    unnamed x2, local copies, waits for them, and re-layouts  2.77 us

profile of v1, /device:TPU:1, one launch (start us, length us, event | category | flops | bytes accessed | tf_op | source)
XLA Modules:
  0.0 73.3 jit_solution(13922494482588508566)
XLA Ops:
  0.0 1.4 %copy.9.corners = s32[192,4]{1,0:T(8,128)} copy(s32[192,4]{0,1:T(4,128)} %param.12) | data formatting | bytes 6144 | tf_op args[4]
  1.4 70.6 %shard_map.82 = f32[6,576]{1,0:T(8,128)} custom-call(bf16[2,64,1536]{2,1,0:T(8,128)(2,1)} %coeff.1, s32[2,2048]{1,0:T(2,128)} %col_map.1, f32[2,2048]{1,0:T(2,128)} %eigen.1, s32[8]{0:T(128)} %band_ids.1, s32[192,4]{1,0:T(8,128)} %copy.9.corners, bf16[3,256,384]{2,1,0:T(8,128)(2,1)} %constant.6.clone.z_mat, bf16[256,256]{1,0:T(8,128)(2,1)} %constant.7.clone.y_mat, ...), custom_call_target="tpu_custom_call" | custom-call | tf_op jit(solution)/shard_map/pallas_call | solution.py:380
  72.0 1.3 %copy.11 = f32[6,576]{1,0:T(8,128)} copy(f32[6,576]{1,0:T(8,128)} %shard_map.82) | data formatting | bytes 27648

commit v2 on v1

v2 whole, which is shorter than its diff:
```python
import functools

import jax
import jax.numpy as jnp
import ml_dtypes
import numpy as np
from jax import lax
from jax.experimental import pallas as pl
from jax.experimental.pallas import tpu as pltpu
from jax.sharding import PartitionSpec as P

NX = 96
NY = 96
NZ = 192
ZPW = 96
BANDS = 8
COLS = 2048
KPOINTS = 32
NTET = 192

FFT = 32
POOLS = 16
KP = 2
LOCAL = COLS // FFT
PLANES = NZ // FFT
ROWS = 48
GROUP = 4
GROUPS = FFT // GROUP
WIDE = GROUP * LOCAL
PITCH = 2 * ROWS + 8
BATCH = 2
BATCHES = PLANES // BATCH
SMEARING = 0.1
MESH = pl.DeviceIdType.MESH
F32 = jnp.float32
BF16 = jnp.bfloat16
NT = (((1,), (1,)), ((), ()))


def phase_parts(frequencies, positions, period):
    product = frequencies[:, None] % period * positions[None, :] % period
    phases = np.float32(2.0 * np.pi / period) * product.astype(np.float32)
    return np.cos(phases), np.sin(phases)


def z_matrices():
    cosine, sine = phase_parts(np.arange(ZPW) - ZPW // 2, np.arange(NZ), NZ)
    full = np.zeros((ZPW, 2, NZ, 2), np.float32)
    full[:, 0, :, 0] = cosine
    full[:, 0, :, 1] = sine
    full[:, 1, :, 0] = -sine
    full[:, 1, :, 1] = cosine
    full = full.reshape(2 * ZPW, FFT, PLANES * 2).transpose(1, 2, 0)
    result = np.zeros((3, FFT, 8, 2, 2 * ZPW), np.float32)
    result[0, :, :, 0] = full[:, :8]
    result[1, :, :, 1] = full[:, :8]
    result[2, :, :4, 0] = full[:, 8:]
    result[2, :, 4:, 1] = full[:, 8:]
    return result.reshape(3 * FFT * 8, 4 * ZPW).astype(ml_dtypes.bfloat16)


def y_matrix():
    cosine, sine = phase_parts(np.arange(NY), np.arange(NY), NY)
    result = np.zeros((2, 128, 2, 128), np.float32)
    result[0, :NY, 0, :NY] = cosine
    result[0, :NY, 1, :NY] = sine
    result[1, :NY, 0, :NY] = -sine
    result[1, :NY, 1, :NY] = cosine
    return result.reshape(256, 256).astype(ml_dtypes.bfloat16)


def x_matrix():
    cosine, sine = phase_parts(np.arange(NX), np.arange(NX), NX)
    result = np.zeros((2, 2, 4, 2, 8, 2, NX), np.float32)
    for core in range(2):
        for chip in range(4):
            for high in range(2):
                owner = (high * 4 + chip) * 2 + core
                mine = slice(owner * 6, owner * 6 + 6)
                result[0, core, chip, high, :6, 0] = cosine[:, mine].T
                result[0, core, chip, high, :6, 1] = -sine[:, mine].T
                result[1, core, chip, high, :6, 0] = sine[:, mine].T
                result[1, core, chip, high, :6, 1] = cosine[:, mine].T
    return result.reshape(256, 2 * NX).astype(ml_dtypes.bfloat16)


def iota(shape, dim):
    return lax.broadcasted_iota(jnp.int32, shape, dim).astype(F32)


def onehot(condition):
    return jnp.where(condition, 1.0, 0.0).astype(BF16)


def dot(a, b):
    return jnp.dot(a, b, preferred_element_type=F32)


def dot_nt(a, b):
    return lax.dot_general(a, b, NT, preferred_element_type=F32)


def wait_bytes(ref, sem):
    pltpu.make_async_copy(ref, ref, sem).wait()


def kernel(
    coeff, col_map, eigen, band_ids, corners, z_mat, y_mat, x_mat, out,
    send, recv, own_levels, levels, weights, ranks, places, block_v, block_s,
    sorter, windows, columns, ordered, ordered_b, grid, field, density,
    in_core, half, in_x, quarter, in_z,
    send_sem, recv_sem, local_sem, level_sem, core_sem, x_sem, z_sem,
):
    fft = lax.axis_index("fft")
    pool = lax.axis_index("kpool")
    core = pool % 2
    chip = pool // 2 % 4
    high = pool // 8

    barrier = pltpu.get_barrier_semaphore()

    def greet_fft(step, carry):
        pl.semaphore_signal(
            barrier, inc=1, device_id={"fft": (fft + step) % FFT}, device_id_type=MESH
        )
        return carry

    def greet_pool(step, carry):
        pl.semaphore_signal(
            barrier, inc=1, device_id={"kpool": (pool + step) % POOLS}, device_id_type=MESH
        )
        return carry

    lax.fori_loop(1, FFT, greet_fft, 0)
    lax.fori_loop(1, POOLS, greet_pool, 0)

    def z_step(k):
        groups = []
        for pair in range(2):
            both = jnp.concatenate(
                [coeff[k, :, (2 * h + pair) * 384 : (2 * h + pair + 1) * 384] for h in range(2)],
                axis=0,
            )
            parts = dot_nt(z_mat[...], both).reshape(3, FFT, 8, 128)
            groups.extend(parts[part] for part in range(3))
        for tile in range(3):
            joined = jnp.concatenate([groups[2 * tile], groups[2 * tile + 1]], axis=1)
            send[k, :, 16 * tile : 16 * tile + 16, :] = joined.astype(BF16)

    def send_columns(k):
        def one(step, carry):
            target = (fft + step) % FFT
            pltpu.make_async_remote_copy(
                src_ref=send.at[k, target],
                dst_ref=recv.at[k, fft],
                send_sem=send_sem.at[k],
                recv_sem=recv_sem.at[k, fft // GROUP],
                device_id={"fft": target},
                device_id_type=MESH,
            ).start()
            return carry

        lax.fori_loop(1, FFT, one, 0)
        pltpu.make_async_copy(send.at[k, fft], recv.at[k, fft], local_sem.at[k]).start()

    z_step(0)
    pl.semaphore_wait(barrier, FFT - 1 + POOLS - 1)
    send_columns(0)

    band = lax.broadcasted_iota(jnp.int32, (BANDS, 2048), 0)
    chosen = jnp.zeros((BANDS, 2048), jnp.int32)
    for n in range(BANDS):
        chosen = jnp.where(band == n, band_ids[n], chosen)
    found = chosen == lax.broadcasted_iota(jnp.int32, (BANDS, 2048), 1)
    lane = lax.broadcasted_iota(jnp.int32, (BANDS, 128), 1)
    table = jnp.zeros((BANDS, 128), F32)
    for k in range(KP):
        picked = jnp.sum(jnp.where(found, eigen[k : k + 1, :], 0.0), axis=1, keepdims=True)
        table = jnp.where(lane == pool * KP + k, picked, table)
    own_levels[...] = table

    def send_levels(step, carry):
        pltpu.make_async_remote_copy(
            src_ref=own_levels,
            dst_ref=levels.at[pool],
            send_sem=level_sem.at[0],
            recv_sem=level_sem.at[1],
            device_id={"kpool": (pool + step) % POOLS},
            device_id_type=MESH,
        ).start()
        return carry

    lax.fori_loop(1, POOLS, send_levels, 0)
    pltpu.make_async_copy(own_levels, levels.at[pool], local_sem.at[2]).start()

    z_step(1)

    for k in range(KP):
        place = col_map[k : k + 1, :].astype(F32)
        x_of = jnp.floor((place + 0.5) * (1.0 / NY))
        y_of = place - NY * x_of
        rows = iota((128, COLS), 0)
        in_x_row = rows == x_of
        x_hot = onehot(in_x_row)
        y_hot = onehot(rows == y_of)
        taken = dot_nt(x_hot, y_hot)
        first = iota((128, 128), 0)
        second = iota((128, 128), 1)
        taken_b = taken.astype(BF16)
        before = dot(taken_b, onehot(first < second))
        above = dot(onehot(second < first), taken_b)
        start = jnp.sum(above, axis=1, keepdims=True)
        x_from = lax.broadcasted_iota(jnp.int32, (NX, COLS), 0) * NY
        count = jnp.sum(
            jnp.where(col_map[k : k + 1, :] < x_from, 1, 0), axis=1, keepdims=True
        )
        block_v[k] = jnp.broadcast_to(jnp.minimum(count >> 7, COLS // 128 - 1), (NX, 128))
        block = jnp.minimum(jnp.floor(start * (1.0 / 128)), COLS // 128 - 1.0)
        places[k] = jnp.where(taken > 0.5, start + before - 128.0 * block, -1.0).astype(jnp.int32)
        within = dot(before.astype(BF16), y_hot)
        rank = jnp.sum(jnp.where(in_x_row, start + within, 0.0), axis=0, keepdims=True)
        for group in range(GROUPS):
            ranks[k, group : group + 1, :] = rank[:, WIDE * group : WIDE * (group + 1)]
    block_copy = pltpu.make_async_copy(block_v, block_s, local_sem.at[3])
    block_copy.start()

    for k in range(KP):
        def sorter_rows(step, carry, k=k):
            group = step // 8
            part = step % 8
            rows = lax.broadcasted_iota(jnp.int32, (256, WIDE), 0) + part * 256
            sorter[
                k,
                pl.ds(pl.multiple_of(part * 256, 256), 256),
                pl.ds(pl.multiple_of(group * WIDE, WIDE), WIDE),
            ] = onehot(rows.astype(F32) == ranks[k, pl.ds(group, 1), :])
            return carry

        lax.fori_loop(0, GROUPS * 8, sorter_rows, 0)

        def window(step, carry, k=k):
            windows[k, step] = onehot(
                lax.broadcasted_iota(jnp.int32, (256, 128), 0)
                == places[k, pl.ds(2 * step + 1, 1), :]
            )
            return carry

        lax.fori_loop(0, NX // 2, window, 0)

    wait_bytes(send.at[0, pl.ds(0, FFT - 1)], send_sem.at[0])
    send_columns(1)

    def find_weights():
        wait_bytes(levels.at[pl.ds(0, POOLS - 1)], level_sem.at[1])
        pltpu.make_async_copy(own_levels, levels.at[pool], local_sem.at[2]).wait()
        every = levels[0]
        for j in range(1, POOLS):
            every = every + levels[j]
        kpoint = lax.broadcasted_iota(jnp.int32, (128, NTET), 0)
        member = jnp.zeros((128, NTET), F32)
        for c in range(4):
            member = member + jnp.where(corners[c : c + 1, :] == kpoint, 1.0, 0.0)
        mean = 0.25 * jnp.dot(
            every, member, precision=lax.Precision.HIGHEST, preferred_element_type=F32
        )
        occupied = jax.nn.sigmoid((0.0 - mean) / SMEARING)
        for k in range(KP):
            mine = jnp.zeros((1, NTET), F32)
            for c in range(4):
                mine = mine + jnp.where(corners[c : c + 1, :] == pool * KP + k, 1.0, 0.0)
            weight = jnp.sum(mine * occupied, axis=1, keepdims=True) * (2.0 / (4 * NTET))
            weights[k * BANDS : (k + 1) * BANDS, :] = jnp.broadcast_to(weight, (BANDS, 128))

    low = lax.broadcasted_iota(jnp.int32, (ROWS, 128), 1) < LOCAL

    def gather_group(k, group):
        upper, lower = [], []
        for pair in range(GROUP // 2):
            even = recv[k, GROUP * group + 2 * pair].astype(F32)
            odd = recv[k, GROUP * group + 2 * pair + 1].astype(F32)
            upper.append(jnp.where(low, even, pltpu.roll(odd, LOCAL, 1)))
            lower.append(jnp.where(low, pltpu.roll(even, LOCAL, 1), odd))
        return jnp.concatenate(
            [jnp.concatenate(upper, axis=1), jnp.concatenate(lower, axis=1)], axis=0
        ).astype(BF16)

    def each_group(k, work):
        def one(step, carry):
            group = (fft // GROUP + GROUPS - step) % GROUPS
            wait_bytes(recv.at[k, pl.ds(0, GROUP)], recv_sem.at[k, group])
            work(group)
            return carry

        lax.fori_loop(1, GROUPS, one, 0)
        group = fft // GROUP
        wait_bytes(recv.at[k, pl.ds(0, GROUP - 1)], recv_sem.at[k, group])
        pltpu.make_async_copy(send.at[k, fft], recv.at[k, fft], local_sem.at[k]).wait()
        work(group)

    def order_as_they_come(k):
        ordered[...] = jnp.zeros_like(ordered)

        def work(group):
            part_columns = gather_group(k, group)
            at = pl.ds(pl.multiple_of(group * WIDE, WIDE), WIDE)
            for part in range(8):
                moved = dot_nt(part_columns, sorter[k, 256 * part : 256 * (part + 1), at])
                ordered[2 * part] += moved[:, :128]
                ordered[2 * part + 1] += moved[:, 128:]

        each_group(k, work)

    def order_at_once(k):
        def work(group):
            columns[:, pl.ds(pl.multiple_of(group * WIDE, WIDE), WIDE)] = gather_group(k, group)

        each_group(k, work)

        def chunk(step, carry):
            at = pl.ds(pl.multiple_of(step * 256, 256), 256)
            moved = dot_nt(columns[...], sorter[k, at, :])
            ordered[2 * step] = moved[:, :128]
            ordered[2 * step + 1] = moved[:, 128:]
            return carry

        lax.fori_loop(0, COLS // 256, chunk, 0, unroll=2)

    def fill_grid(k):
        for block in range(COLS // 128 + 1):
            ordered_b[block] = ordered[block].astype(BF16)

        def two(step, carry):
            x = 2 * step
            block = block_s[k, x, 0]
            place = jnp.broadcast_to(places[k, pl.ds(x, 1), :], (2 * ROWS, 128))
            lane = place & 127
            near = jnp.take_along_axis(ordered[block], lane, axis=1, mode="promise_in_bounds")
            far = jnp.take_along_axis(ordered[block + 1], lane, axis=1, mode="promise_in_bounds")
            row = jnp.where(place < 0, 0.0, jnp.where(place < 128, near, far))
            grid[pl.ds(x * PITCH, 2 * ROWS), :] = row
            block = block_s[k, x + 1, 0]
            both = jnp.concatenate([ordered_b[block], ordered_b[block + 1]], axis=1)
            grid[pl.ds(x * PITCH + PITCH, 2 * ROWS), :] = dot(both, windows[k, step])
            return carry

        lax.fori_loop(0, NX // 2, two, 0, unroll=4)

    def add_plane(k, p):
        for pair in range(BANDS // 2):
            row = pair * 24 + (2 * p if p < 4 else 16 + 2 * (p - 4))
            apart = 8 if p < 4 else 4
            for e in range(2):
                for c in range(2):
                    field[(2 * pair + e) * NX : (2 * pair + e + 1) * NX, 128 * c : 128 * (c + 1)] = (
                        grid[pl.ds(row + apart * e + c, NX, stride=PITCH), :].astype(BF16)
                    )
        along_y = dot(field[...], y_mat[...]).astype(BF16)
        total = density[p]
        for pair in range(BANDS // 2):
            one, two = (
                along_y[(2 * pair + e) * NX : (2 * pair + e + 1) * NX] for e in range(2)
            )
            turned = jnp.concatenate(
                [
                    jnp.concatenate([one[:, :128], two[:, :128]], axis=1),
                    jnp.concatenate([one[:, 128:], two[:, 128:]], axis=1),
                ],
                axis=0,
            )
            psi = dot(x_mat[...], turned)
            power = psi[:128] * psi[:128] + psi[128:] * psi[128:]
            at = k * BANDS + 2 * pair
            total = total + (
                weights[at : at + 1, :] * power[:, :128]
                + weights[at + 1 : at + 2, :] * power[:, 128:]
            )
        density[p] = total

    def planes(batch):
        return pl.ds(BATCH * batch, BATCH)

    def rows_of(index, size):
        return pl.ds(pl.multiple_of(index * size, size), size)

    def core_copy(batch):
        return pltpu.make_async_remote_copy(
            src_ref=density.at[planes(batch), rows_of(1 - core, 64), :],
            dst_ref=in_core.at[planes(batch)],
            send_sem=core_sem.at[0, batch],
            recv_sem=core_sem.at[1, batch],
            device_id={"kpool": pool + 1 - 2 * core},
            device_id_type=MESH,
        )

    def x_copies(batch):
        copies = []
        for step in range(1, 4):
            target = (chip + step) % 4
            copies.append(
                pltpu.make_async_remote_copy(
                    src_ref=half.at[planes(batch), rows_of(target, 16), :],
                    dst_ref=in_x.at[step - 1, planes(batch)],
                    send_sem=x_sem.at[0, step - 1, batch],
                    recv_sem=x_sem.at[1, step - 1, batch],
                    device_id={"kpool": (high * 4 + target) * 2 + core},
                    device_id_type=MESH,
                )
            )
        return copies

    def z_copy(batch):
        return pltpu.make_async_remote_copy(
            src_ref=quarter.at[planes(batch), rows_of(1 - high, 8), :],
            dst_ref=in_z.at[planes(batch)],
            send_sem=z_sem.at[0, batch],
            recv_sem=z_sem.at[1, batch],
            device_id={"kpool": pool + 8 - 16 * high},
            device_id_type=MESH,
        )

    def sum_core(batch):
        core_copy(batch).wait_recv()
        at = planes(batch)
        half[at] = density[at, rows_of(core, 64), :] + in_core[at]
        for copy in x_copies(batch):
            copy.start()

    def sum_x(batch):
        at = planes(batch)
        total = half[at, rows_of(chip, 16), :]
        for step, copy in enumerate(x_copies(batch)):
            copy.wait_recv()
            total = total + in_x[step, at]
        quarter[at] = total
        z_copy(batch).start()

    def sum_z(batch):
        z_copy(batch).wait_recv()
        at = planes(batch)
        total = quarter[at, rows_of(high, 8), :] + in_z[at]
        for i in range(6):
            out[BATCH * batch : BATCH * (batch + 1), NY * i : NY * (i + 1)] = total[:, i, :NY]

    density[...] = jnp.zeros_like(density)
    block_copy.wait()

    order_as_they_come(0)
    find_weights()
    fill_grid(0)
    for p in range(PLANES):
        add_plane(0, p)
    order_at_once(1)
    fill_grid(1)
    for step in range(BATCHES + 2):
        if step < BATCHES:
            for p in range(BATCH):
                add_plane(1, BATCH * step + p)
            core_copy(step).start()
        if 1 <= step <= BATCHES:
            sum_core(step - 1)
        if step >= 2:
            sum_x(step - 2)
    for batch in range(BATCHES):
        sum_z(batch)

    for batch in range(BATCHES):
        core_copy(batch).wait_send()
        for copy in x_copies(batch):
            copy.wait_send()
        z_copy(batch).wait_send()
    wait_bytes(send.at[1, pl.ds(0, FFT - 1)], send_sem.at[1])
    wait_bytes(levels.at[pl.ds(0, POOLS - 1)], level_sem.at[0])


def per_device(coeff, col_map, eigen, band_ids, tet_corners):
    vmem = pl.BlockSpec(memory_space=pltpu.VMEM)
    smem = pl.BlockSpec(memory_space=pltpu.SMEM)
    return pl.pallas_call(
        kernel,
        out_shape=jax.ShapeDtypeStruct((PLANES, 6 * NY), F32),
        in_specs=[vmem, vmem, vmem, smem, vmem, vmem, vmem, vmem],
        out_specs=vmem,
        scratch_shapes=[
            pltpu.VMEM((KP, FFT, ROWS, 128), BF16),
            pltpu.VMEM((KP, FFT, ROWS, 128), BF16),
            pltpu.VMEM((8, 128), F32),
            pltpu.VMEM((POOLS, 8, 128), F32),
            pltpu.VMEM((KP * BANDS, 128), F32),
            pltpu.VMEM((KP, GROUPS, WIDE), F32),
            pltpu.VMEM((KP, 128, 128), jnp.int32),
            pltpu.VMEM((KP, NX, 128), jnp.int32),
            pltpu.SMEM((KP, NX, 128), jnp.int32),
            pltpu.VMEM((KP, COLS, COLS), BF16),
            pltpu.VMEM((KP, NX // 2, 256, 128), BF16),
            pltpu.VMEM((2 * ROWS, COLS), BF16),
            pltpu.VMEM((COLS // 128 + 1, 2 * ROWS, 128), F32),
            pltpu.VMEM((COLS // 128 + 1, 2 * ROWS, 128), BF16),
            pltpu.VMEM((NX * PITCH, 128), F32),
            pltpu.VMEM((BANDS * NX, 256), BF16),
            pltpu.VMEM((PLANES, 128, 128), F32),
            pltpu.VMEM((PLANES, 64, 128), F32),
            pltpu.VMEM((PLANES, 64, 128), F32),
            pltpu.VMEM((3, PLANES, 16, 128), F32),
            pltpu.VMEM((PLANES, 16, 128), F32),
            pltpu.VMEM((PLANES, 8, 128), F32),
            pltpu.SemaphoreType.DMA((KP,)),
            pltpu.SemaphoreType.DMA((KP, GROUPS)),
            pltpu.SemaphoreType.DMA((4,)),
            pltpu.SemaphoreType.DMA((2,)),
            pltpu.SemaphoreType.DMA((2, BATCHES)),
            pltpu.SemaphoreType.DMA((2, 3, BATCHES)),
            pltpu.SemaphoreType.DMA((2, BATCHES)),
        ],
        compiler_params=pltpu.CompilerParams(
            collective_id=0, has_side_effects=True, vmem_limit_bytes=56 * 1024 * 1024
        ),
    )(
        coeff, col_map, eigen, band_ids, tet_corners.T,
        jnp.asarray(z_matrices()), jnp.asarray(y_matrix()), jnp.asarray(x_matrix()),
    )


def solution(mesh):
    in_specs = (P("kpool", "fft", None), P("kpool", None), P("kpool", None), P(), P())
    out_specs = P("fft", "kpool")
    return jax.shard_map(
        per_device, mesh=mesh, in_specs=in_specs, out_specs=out_specs, check_vma=False
    )
```

time: 73.6 us -> 66.2 us (0.90)
  Pallas kernels: 70.6 us -> 64.5 us
  local copies, waits for them, and re-layouts: 2.77 us -> 1.34 us
    pallas_call x1, Pallas kernels: 70.6 us -> 64.5 us  [per_device(): pl.pallas_call(kernel, out_shape=jax.ShapeDtypeStruct((PLANES, 6 * NY), F...]
    unnamed x2 -> x1, local copies, waits for them, and re-layouts: 2.77 us -> 1.34 us
where the time goes in v2:
time: 66.2 us; the launch traced here: 65.8 us
  Pallas kernels  64.5 us (97%)
  local copies, waits for them, and re-layouts  1.34 us (2%)
    pallas_call x1, Pallas kernels, per_device(): pl.pallas_call(kernel, out_shape=jax.ShapeDtypeStruct((PLANES, 6 * NY), F...  64.5 us
    unnamed x1, local copies, waits for them, and re-layouts  1.34 us

profile of v2, /device:TPU:1, one launch (start us, length us, event | category | flops | bytes accessed | tf_op | source)
XLA Modules:
  0.0 65.8 jit_solution(13257102471094577338)
XLA Ops:
  0.0 64.5 %shard_map.82 = f32[6,576]{1,0:T(8,128)} custom-call(bf16[2,64,1536]{2,1,0:T(8,128)(2,1)} %coeff.1, s32[2,2048]{1,0:T(2,128)} %col_map.1, f32[2,2048]{1,0:T(2,128)} %eigen.1, s32[8]{0:T(128)} %band_ids.1, s32[4,192]{1,0:T(4,128)} %bitcast.1, bf16[768,384]{1,0:T(8,128)(2,1)} %constant.6.clone.z_mat, bf16[256,256]{1,0:T(8,128)(2,1)} %constant.7.clone.y_mat, ...), custom_call_target="tpu_custom_call" | custom-call | tf_op jit(solution)/shard_map/pallas_call | solution.py:478
  64.5 1.3 %copy.10 = f32[6,576]{1,0:T(8,128)} copy(f32[6,576]{1,0:T(8,128)} %shard_map.82) | data formatting | bytes 27648

commit v3 on v2

--- a/solution.py
+++ b/solution.py
@@ -29,6 +29,7 @@
 WIDE = GROUP * LOCAL
 PITCH = 2 * ROWS + 8
 BATCH = 2
+OWNED = 6
 BATCHES = PLANES // BATCH
 SMEARING = 0.1
 MESH = pl.DeviceIdType.MESH
@@ -108,8 +109,7 @@
     coeff, col_map, eigen, band_ids, corners, z_mat, y_mat, x_mat, out,
     send, recv, own_levels, levels, weights, ranks, places, block_v, block_s,
     sorter, windows, columns, ordered, ordered_b, grid, field, density,
-    in_core, half, in_x, quarter, in_z,
-    send_sem, recv_sem, local_sem, level_sem, core_sem, x_sem, z_sem,
+    terms, send_sem, recv_sem, local_sem, level_sem, sum_sem,
 ):
     fft = lax.axis_index("fft")
     pool = lax.axis_index("kpool")
@@ -379,65 +379,33 @@
     def planes(batch):
         return pl.ds(BATCH * batch, BATCH)
 
-    def rows_of(index, size):
-        return pl.ds(pl.multiple_of(index * size, size), size)
-
-    def core_copy(batch):
-        return pltpu.make_async_remote_copy(
-            src_ref=density.at[planes(batch), rows_of(1 - core, 64), :],
-            dst_ref=in_core.at[planes(batch)],
-            send_sem=core_sem.at[0, batch],
-            recv_sem=core_sem.at[1, batch],
-            device_id={"kpool": pool + 1 - 2 * core},
-            device_id_type=MESH,
-        )
-
-    def x_copies(batch):
+    def rows_of(owner):
+        place = (owner % 2) * 8 + (owner // 2 % 4) * 2 + owner // 8
+        return pl.ds(pl.multiple_of(place * 8, 8), OWNED)
+
+    def term_copies(batch):
         copies = []
-        for step in range(1, 4):
-            target = (chip + step) % 4
+        for step in range(1, POOLS):
+            turn = POOLS - step
+            owner = ((high + turn // 8) % 2) * 8 + (chip * 2 + core + turn) % 8
             copies.append(
                 pltpu.make_async_remote_copy(
-                    src_ref=half.at[planes(batch), rows_of(target, 16), :],
-                    dst_ref=in_x.at[step - 1, planes(batch)],
-                    send_sem=x_sem.at[0, step - 1, batch],
-                    recv_sem=x_sem.at[1, step - 1, batch],
-                    device_id={"kpool": (high * 4 + target) * 2 + core},
+                    src_ref=density.at[planes(batch), rows_of(owner), :],
+                    dst_ref=terms.at[step - 1, planes(batch)],
+                    send_sem=sum_sem.at[0, batch],
+                    recv_sem=sum_sem.at[1, batch],
+                    device_id={"kpool": owner},
                     device_id_type=MESH,
                 )
             )
         return copies
 
-    def z_copy(batch):
-        return pltpu.make_async_remote_copy(
-            src_ref=quarter.at[planes(batch), rows_of(1 - high, 8), :],
-            dst_ref=in_z.at[planes(batch)],
-            send_sem=z_sem.at[0, batch],
-            recv_sem=z_sem.at[1, batch],
-            device_id={"kpool": pool + 8 - 16 * high},
-            device_id_type=MESH,
-        )
-
-    def sum_core(batch):
-        core_copy(batch).wait_recv()
+    def sum_terms(batch):
         at = planes(batch)
-        half[at] = density[at, rows_of(core, 64), :] + in_core[at]
-        for copy in x_copies(batch):
-            copy.start()
-
-    def sum_x(batch):
-        at = planes(batch)
-        total = half[at, rows_of(chip, 16), :]
-        for step, copy in enumerate(x_copies(batch)):
-            copy.wait_recv()
-            total = total + in_x[step, at]
-        quarter[at] = total
-        z_copy(batch).start()
-
-    def sum_z(batch):
-        z_copy(batch).wait_recv()
-        at = planes(batch)
-        total = quarter[at, rows_of(high, 8), :] + in_z[at]
+        wait_bytes(terms.at[:, at], sum_sem.at[1, batch])
+        total = density[at, rows_of(pool), :]
+        for step in range(POOLS - 1):
+            total = total + terms[step, at]
         for i in range(6):
             out[BATCH * batch : BATCH * (batch + 1), NY * i : NY * (i + 1)] = total[:, i, :NY]
 
@@ -451,23 +419,16 @@
         add_plane(0, p)
     order_at_once(1)
     fill_grid(1)
-    for step in range(BATCHES + 2):
-        if step < BATCHES:
-            for p in range(BATCH):
-                add_plane(1, BATCH * step + p)
-            core_copy(step).start()
-        if 1 <= step <= BATCHES:
-            sum_core(step - 1)
-        if step >= 2:
-            sum_x(step - 2)
     for batch in range(BATCHES):
-        sum_z(batch)
-
+        for p in range(BATCH):
+            add_plane(1, BATCH * batch + p)
+        for copy in term_copies(batch):
+            copy.start()
     for batch in range(BATCHES):
-        core_copy(batch).wait_send()
-        for copy in x_copies(batch):
-            copy.wait_send()
-        z_copy(batch).wait_send()
+        sum_terms(batch)
+
+    for batch in range(BATCHES):
+        wait_bytes(terms.at[:, planes(batch)], sum_sem.at[0, batch])
     wait_bytes(send.at[1, pl.ds(0, FFT - 1)], send_sem.at[1])
     wait_bytes(levels.at[pl.ds(0, POOLS - 1)], level_sem.at[0])
 
@@ -498,17 +459,11 @@
             pltpu.VMEM((NX * PITCH, 128), F32),
             pltpu.VMEM((BANDS * NX, 256), BF16),
             pltpu.VMEM((PLANES, 128, 128), F32),
-            pltpu.VMEM((PLANES, 64, 128), F32),
-            pltpu.VMEM((PLANES, 64, 128), F32),
-            pltpu.VMEM((3, PLANES, 16, 128), F32),
-            pltpu.VMEM((PLANES, 16, 128), F32),
-            pltpu.VMEM((PLANES, 8, 128), F32),
+            pltpu.VMEM((POOLS - 1, PLANES, OWNED, 128), F32),
             pltpu.SemaphoreType.DMA((KP,)),
             pltpu.SemaphoreType.DMA((KP, GROUPS)),
             pltpu.SemaphoreType.DMA((4,)),
             pltpu.SemaphoreType.DMA((2,)),
-            pltpu.SemaphoreType.DMA((2, BATCHES)),
-            pltpu.SemaphoreType.DMA((2, 3, BATCHES)),
             pltpu.SemaphoreType.DMA((2, BATCHES)),
         ],
         compiler_params=pltpu.CompilerParams(

time: 66.2 us -> 64 us (0.967)
  Pallas kernels: 64.5 us -> 62.4 us
    pallas_call x1, Pallas kernels: 64.5 us -> 62.4 us  [per_device(): pl.pallas_call(kernel, out_shape=jax.ShapeDtypeStruct((PLANES, 6 * NY), F...]
where the time goes in v3:
time: 64 us; the launch traced here: 63.7 us
  Pallas kernels  62.4 us (98%)
  local copies, waits for them, and re-layouts  1.34 us (2%)
    pallas_call x1, Pallas kernels, per_device(): pl.pallas_call(kernel, out_shape=jax.ShapeDtypeStruct((PLANES, 6 * NY), F...  62.4 us
    unnamed x1, local copies, waits for them, and re-layouts  1.34 us

profile of v3, /device:TPU:1, one launch (start us, length us, event | category | flops | bytes accessed | tf_op | source)
XLA Modules:
  0.0 63.7 jit_solution(11337500811485646611)
XLA Ops:
  0.0 62.4 %shard_map.82 = f32[6,576]{1,0:T(8,128)} custom-call(bf16[2,64,1536]{2,1,0:T(8,128)(2,1)} %coeff.1, s32[2,2048]{1,0:T(2,128)} %col_map.1, f32[2,2048]{1,0:T(2,128)} %eigen.1, s32[8]{0:T(128)} %band_ids.1, s32[4,192]{1,0:T(4,128)} %bitcast.1, bf16[768,384]{1,0:T(8,128)(2,1)} %constant.6.clone.z_mat, bf16[256,256]{1,0:T(8,128)(2,1)} %constant.7.clone.y_mat, ...), custom_call_target="tpu_custom_call" | custom-call | tf_op jit(solution)/shard_map/pallas_call | solution.py:439
  62.4 1.3 %copy.10 = f32[6,576]{1,0:T(8,128)} copy(f32[6,576]{1,0:T(8,128)} %shard_map.82) | data formatting | bytes 27648

commit v4 on v3

--- a/solution.py
+++ b/solution.py
@@ -247,7 +247,6 @@
 
         lax.fori_loop(0, NX // 2, window, 0)
 
-    wait_bytes(send.at[0, pl.ds(0, FFT - 1)], send_sem.at[0])
     send_columns(1)
 
     def find_weights():
@@ -429,7 +428,8 @@
 
     for batch in range(BATCHES):
         wait_bytes(terms.at[:, planes(batch)], sum_sem.at[0, batch])
-    wait_bytes(send.at[1, pl.ds(0, FFT - 1)], send_sem.at[1])
+    for k in range(KP):
+        wait_bytes(send.at[k, pl.ds(0, FFT - 1)], send_sem.at[k])
     wait_bytes(levels.at[pl.ds(0, POOLS - 1)], level_sem.at[0])
 
 

time: 64 us -> 63.9 us (level)
  no operation moved by 1% of the time
where the time goes in v4:
time: 63.9 us; the launch traced here: 63.7 us
  Pallas kernels  62.4 us (98%)
  local copies, waits for them, and re-layouts  1.34 us (2%)
    pallas_call x1, Pallas kernels, per_device(): pl.pallas_call(kernel, out_shape=jax.ShapeDtypeStruct((PLANES, 6 * NY), F...  62.4 us
    unnamed x1, local copies, waits for them, and re-layouts  1.34 us

profile of v4, /device:TPU:1, one launch (start us, length us, event | category | flops | bytes accessed | tf_op | source)
XLA Modules:
  0.0 63.7 jit_solution(15605845100793234253)
XLA Ops:
  0.0 62.4 %shard_map.82 = f32[6,576]{1,0:T(8,128)} custom-call(bf16[2,64,1536]{2,1,0:T(8,128)(2,1)} %coeff.1, s32[2,2048]{1,0:T(2,128)} %col_map.1, f32[2,2048]{1,0:T(2,128)} %eigen.1, s32[8]{0:T(128)} %band_ids.1, s32[4,192]{1,0:T(4,128)} %bitcast.1, bf16[768,384]{1,0:T(8,128)(2,1)} %constant.6.clone.z_mat, bf16[256,256]{1,0:T(8,128)(2,1)} %constant.7.clone.y_mat, ...), custom_call_target="tpu_custom_call" | custom-call | tf_op jit(solution)/shard_map/pallas_call | solution.py:439
  62.4 1.3 %copy.10 = f32[6,576]{1,0:T(8,128)} copy(f32[6,576]{1,0:T(8,128)} %shard_map.82) | data formatting | bytes 27648
